TPU v7x, 32 devices: a whole 2x2x4 slice. The times are simulated.
32 devices in a mesh: sites: 2 (over x), blk: 16 (over z, y, core).
Axes of the slice: x: 2, y: 2, z: 4, core: 2. Of those that a mesh axis runs over, the one named last changes fastest.
Arguments:
- green: bfloat16 [4096, 2, 2, 256], P(('sites', 'blk')), parts along dimension 0, may hold values from -9 to 9
- slip: bfloat16 [2, 256, 8, 128], P(None, 'blk'), may hold values from 0.049804688 to 1
- onset_bin: int32 [2, 256, 128], P(None, 'blk'), may hold values from 0 to 3
- item_helper: int32 [2, 256, 1], P(None, 'blk'), may hold values from 0 to 15; in each aligned block of 16 rows (0 to 15, 16 to 31, ..., all dimensions but the last counted through in order) at most 2 rows name the same one
- item_rupture: int32 [2, 256], P(None, 'blk'), may hold values from 0 to 3
- base_shift: int32 [2, 64, 8], P(None, 'blk'), may hold values from 0 to 511
- rupture_rate: float32 [2, 64], P(None, 'blk'), may hold values from 0.00046875 to 1.5625, as said below
Outputs:
- seismograms: float32 [2, 128, 8, 2, 512], P(None, ('sites', 'blk')), parts along dimension 1
- site_log_power: float32 [4, 256], P('sites'), parts along dimension 0
There are 2 independent parts, one for each index of `sites`. A program takes and returns all parts, laid end to end along the dimension named above; an argument that names none is the same for every part. Nothing has to cross between parts.
Inputs may be any that keep to these rules, and one draw needn't show every extreme that they name: `item_helper`: in each batch, the 16 segments of one device name no helper more than 2 times. `rupture_rate`: positive rates.
All inputs are finite; a program needn't handle non-finite values.
Results may differ from a plain program's by a relative error of at most 0.0015.
Values may be sent and summed in bfloat16 or wider, within the bound.
A program may use at most 128 MiB of HBM per device.

v0:
```python
import math

import jax
import jax.numpy as jnp
from jax import lax
from jax.sharding import PartitionSpec as P

FREQS = 256
COMPS = 2
VARIATIONS = 8
ONSET_BINS = 4
BIN_LAG = 9
BATCHES = 2
CAPACITY = 2
SAMPLES = 512


def phase_tables():
    frequency = jnp.arange(FREQS, dtype=jnp.int32)
    bins_all = jnp.arange(ONSET_BINS, dtype=jnp.int32)
    turns = bins_all[:, None] * BIN_LAG * frequency[None, :] % SAMPLES
    angles = 2.0 * math.pi / SAMPLES * turns.astype(jnp.float32)
    return (jnp.cos(angles), jnp.sin(angles))


def inverse_table():
    frequency = jnp.arange(FREQS, dtype=jnp.int32)
    sample = jnp.arange(SAMPLES, dtype=jnp.int32)
    angles = (
        2.0
        * math.pi
        / SAMPLES
        * (frequency[:, None] * sample[None, :] % SAMPLES).astype(jnp.float32)
    )
    weight = jnp.where(frequency == 0, 1.0 / SAMPLES, 2.0 / SAMPLES).astype(jnp.float32)[:, None]
    return jnp.concatenate([weight * jnp.cos(angles), -weight * jnp.sin(angles)], axis=0)


def slot_numbers(helpers):
    counted = helpers.shape[0]
    same_helper = helpers[:, None] == helpers[None, :]
    earlier = (
        jnp.arange(counted, dtype=jnp.int32)[None, :]
        < jnp.arange(counted, dtype=jnp.int32)[:, None]
    )
    rank_within = jnp.sum(jnp.logical_and(same_helper, earlier), axis=1)
    return helpers * CAPACITY + rank_within


def contract_slots(green_rows, tables, slip_rows, onset_rows):
    counted = slip_rows.shape[0]
    group_size = math.gcd(counted, 32)
    subfault_count = slip_rows.shape[2]
    cos_rows = tables[0][None, :, None, None, :]
    sin_rows = tables[1][None, :, None, None, :]

    def one_group(pieces):
        slip_group, onset_group = pieces
        binned = (
            lax.broadcasted_iota(jnp.int32, (1, ONSET_BINS, 1, 1), 1)
            == onset_group[:, None, None, :]
        )
        masked = jnp.where(binned, slip_group[:, None], jnp.zeros((), slip_group.dtype))
        masked = masked.reshape(group_size * ONSET_BINS * VARIATIONS, subfault_count)
        summed = jnp.dot(masked, green_rows, preferred_element_type=jnp.float32)
        summed = summed.reshape(group_size, ONSET_BINS, VARIATIONS, COMPS, 2, FREQS)
        real_part = jnp.sum(
            cos_rows * summed[:, :, :, :, 0] + sin_rows * summed[:, :, :, :, 1], axis=1
        )
        imag_part = jnp.sum(
            cos_rows * summed[:, :, :, :, 1] - sin_rows * summed[:, :, :, :, 0], axis=1
        )
        stacked = jnp.stack([real_part, imag_part], axis=3)
        return stacked.reshape(group_size, VARIATIONS, COMPS * 2 * FREQS).astype(jnp.bfloat16)

    shaped = (
        slip_rows.reshape(counted // group_size, group_size, VARIATIONS, subfault_count),
        onset_rows.reshape(counted // group_size, group_size, subfault_count),
    )
    result = lax.map(one_group, shaped)
    return result.reshape(counted, VARIATIONS, COMPS * 2 * FREQS)


def finish_batch(returned, slot_index, rupture_local, shift_rows, rate_rows, inverse):
    total_slots = returned.shape[0]
    rupt_count = shift_rows.shape[0]
    rupture_hot = (
        rupture_local[:, None] == jnp.arange(rupt_count, dtype=jnp.int32)[None, :]
    ).astype(jnp.bfloat16)
    slot_hot = (slot_index[:, None] == jnp.arange(total_slots, dtype=jnp.int32)[None, :]).astype(
        jnp.bfloat16
    )
    selector = lax.dot_general(
        rupture_hot, slot_hot, (((0,), (0,)), ((), ())), preferred_element_type=jnp.float32
    )
    selector = selector.astype(jnp.bfloat16)
    spectrum = jnp.dot(
        selector,
        returned.reshape(total_slots, VARIATIONS * COMPS * 2 * FREQS),
        preferred_element_type=jnp.float32,
    )
    spectrum = spectrum.reshape(rupt_count, VARIATIONS, COMPS, 2, FREQS)
    real_part = spectrum[:, :, :, 0]
    imag_part = spectrum[:, :, :, 1]
    frequency = jnp.arange(FREQS, dtype=jnp.int32)
    turns = shift_rows[:, :, None] * frequency[None, None, :] % SAMPLES
    angles = 2.0 * math.pi / SAMPLES * turns.astype(jnp.float32)
    cos_shift = jnp.cos(angles)[:, :, None, :]
    sin_shift = jnp.sin(angles)[:, :, None, :]
    shifted = jnp.stack(
        [
            real_part * cos_shift + imag_part * sin_shift,
            imag_part * cos_shift - real_part * sin_shift,
        ],
        axis=3,
    )
    seismo = jnp.dot(
        shifted.reshape(rupt_count * VARIATIONS * COMPS, 2 * FREQS),
        inverse,
        precision=lax.Precision.HIGHEST,
    )
    energy = jnp.mean(real_part * real_part + imag_part * imag_part, axis=1)
    power_term = jnp.sum(rate_rows[:, None, None] * energy, axis=0)
    return (seismo.reshape(rupt_count, VARIATIONS, COMPS, SAMPLES), power_term)


def local(green, slip, onset_bin, item_helper, item_rupture, base_shift, rupture_rate):
    devices = lax.axis_size("blk")
    green_rows = green.reshape(green.shape[0], COMPS * 2 * FREQS)
    tables = phase_tables()
    inverse = inverse_table()
    stride = devices * CAPACITY
    slip_tail = slip.shape[2:]
    onset_width = onset_bin.shape[2]
    packed = []
    for batch_index in range(BATCHES):
        slot_index = slot_numbers(item_helper[batch_index, :, 0])
        slip_buffer = (
            jnp.zeros((stride,) + slip_tail, slip.dtype).at[slot_index].set(slip[batch_index])
        )
        onset_buffer = (
            jnp.zeros((stride, onset_width), jnp.int32).at[slot_index].set(onset_bin[batch_index])
        )
        packed.append((slot_index, slip_buffer, onset_buffer))
    returns = []
    slip_all = jnp.stack(
        [entry[1].reshape((devices, CAPACITY) + slip_tail) for entry in packed], axis=1
    )
    slip_all = slip_all.reshape((stride * BATCHES,) + slip_tail)
    onset_all = jnp.stack(
        [entry[2].reshape(devices, CAPACITY, onset_width) for entry in packed], axis=1
    )
    onset_all = onset_all.reshape(stride * BATCHES, onset_width)
    slip_in, onset_in = (
        lax.all_to_all(slip_all, "blk", split_axis=0, concat_axis=0, tiled=True),
        lax.all_to_all(onset_all, "blk", split_axis=0, concat_axis=0, tiled=True),
    )
    partials = contract_slots(green_rows, tables, slip_in, onset_in)
    arrived = lax.all_to_all(partials, "blk", split_axis=0, concat_axis=0, tiled=True)
    arrived = arrived.reshape((devices, BATCHES, CAPACITY) + arrived.shape[1:])
    for batch_index in range(BATCHES):
        returns.append(arrived[:, batch_index].reshape((stride,) + arrived.shape[3:]))
    outputs = []
    power_sum = jnp.zeros((COMPS, FREQS), jnp.float32)
    for batch_index in range(BATCHES):
        seismo, power_term = finish_batch(
            returns[batch_index],
            packed[batch_index][0],
            item_rupture[batch_index],
            base_shift[batch_index],
            rupture_rate[batch_index],
            inverse,
        )
        outputs.append(seismo)
        power_sum = power_sum + power_term
    total_power = lax.psum(power_sum, "blk")
    return (jnp.stack(outputs, axis=0), jnp.log(total_power))


def solution(mesh):
    placed = (
        P(("sites", "blk"), None, None, None),
        P(None, "blk", None, None),
        P(None, "blk", None),
        P(None, "blk", None),
        P(None, "blk"),
        P(None, "blk", None),
        P(None, "blk"),
    )
    return jax.shard_map(
        local,
        mesh=mesh,
        in_specs=placed,
        out_specs=(P(None, ("sites", "blk"), None, None, None), P("sites", None)),
        check_vma=False,
    )
```

profile of v0, /device:TPU:0, one launch (start us, length us, event | category | flops | bytes accessed | tf_op | source)
XLA Modules:
  0.0 102.7 jit_solution(12224998629681560413)
XLA Ops:
  2.2 0.8 scatter_custom_fusion.1
  3.0 0.8 scatter_custom_fusion
  4.4 7.4 %all-to-all-start = ((s32[16,4,128]{2,1,0:T(4,128)}), s32[16,4,128]{2,1,0:T(4,128)S(1)}, u32[]{:S(2)}, u32[]{:S(2)}) async-start(s32[16,4,128]{2,1,0:T(4,128)} %bitcast.15), calls=%async_computation | async-start | bytes 65536 | tf_op jit(solution)/shard_map/all_to_all | solution.py:156
  11.8 0.8 slice_bitcast_fusion.3
  12.6 1.0 scatter_fusion
  13.6 1.0 scatter_fusion.1
  15.3 3.1 %all-to-all-done = s32[16,4,128]{2,1,0:T(4,128)S(1)} async-done(((s32[16,4,128]{2,1,0:T(4,128)}), s32[16,4,128]{2,1,0:T(4,128)S(1)}, u32[]{:S(2)}, u32[]{:S(2)}) %all-to-all-start) | async-done | bytes 32800 | tf_op jit(solution)/shard_map/all_to_all | solution.py:156
  18.4 3.5 %all-to-all-start.1 = ((bf16[64,8,128]{2,1,0:T(8,128)(2,1)}), bf16[64,8,128]{2,1,0:T(8,128)(2,1)S(1)}, u32[]{:S(2)}, u32[]{:S(2)}) async-start(bf16[64,8,128]{2,1,0:T(8,128)(2,1)} %bitcast.21), calls=%async_computation.1 | async-start | bytes 262144 | tf_op jit(solution)/shard_map/all_to_all | solution.py:155
  21.9 1.2 %copy.37 = bf16[128,2,2,256]{0,3,2,1:T(8,128)(2,1)S(1)} copy(bf16[128,2,2,256]{3,2,1,0:T(2,128)(2,1)} %param.9) | data formatting | bytes 524288 | tf_op args[0]
  23.1 6.7 %all-to-all-done.1 = bf16[64,8,128]{2,1,0:T(8,128)(2,1)S(1)} async-done(((bf16[64,8,128]{2,1,0:T(8,128)(2,1)}), bf16[64,8,128]{2,1,0:T(8,128)(2,1)S(1)}, u32[]{:S(2)}, u32[]{:S(2)}) %all-to-all-start.1) | async-done | bytes 131104 | tf_op jit(solution)/shard_map/all_to_all | solution.py:155
  29.8 5.0 %while.13 = (s32[]{:T(128)}, bf16[2,32,8,1024]{3,2,1,0:T(8,128)(2,1)}, s32[2,32,128]{2,1,0:T(8,128)S(1)}, bf16[2,32,8,128]{3,2,1,0:T(8,128)(2,1)S(1)}, bf16[128,...) while((s32[]{:T(128)}, bf16[2,32,8,1024]{3,2,1,0:T(8,128)(2,1)}, ...), condition=%wide.region_9.10_spmd.clone.clone.clone, body=%wide.region_6.9_spmd.clone.clone.clone.sunk | while | flops 272791552 | bytes 11567717 | solution.py:80
  29.9 0.7 fusion.68
  30.7 0.7 add_reduce_fusion.4
  31.5 0.8 constant_dynamic-update-slice_fusion.2
  32.4 0.7 fusion.68
  33.2 0.7 add_reduce_fusion.4
  34.0 0.8 constant_dynamic-update-slice_fusion.2
  34.8 3.8 %all-to-all-start.2 = ((bf16[64,8,1024]{2,1,0:T(8,128)(2,1)}), bf16[64,8,1024]{2,1,0:T(8,128)(2,1)S(1)}, u32[]{:S(2)}, u32[]{:S(2)}) async-start(bf16[64,8,1024]{2,1,0:T(8,128)(2,1)} %bitcast.24), calls=%async_computation.2 | async-start | bytes 2097152 | tf_op jit(solution)/shard_map/all_to_all | solution.py:159
  39.6 2.1 %sine_multiply_fusion = (f32[256,512]{1,0:T(8,128)S(1)}, f32[256,512]{1,0:T(8,128)S(1)}) fusion(f32[256]{0:T(256)S(1)} %fusion.56, f32[256]{0:T(256)S(1)} %compare_select_fusion.2), kind=kLoop, calls=%fused_computation.49 | loop fusion | flops 2097152 | bytes 1050624 | tf_op jit(solution)/shard_map/mul | solution.py:36
  41.7 19.8 %all-to-all-done.2 = bf16[64,8,1024]{2,1,0:T(8,128)(2,1)S(1)} async-done(((bf16[64,8,1024]{2,1,0:T(8,128)(2,1)}), bf16[64,8,1024]{2,1,0:T(8,128)(2,1)S(1)}, u32[]{:S(2)}, u32[]{:S(2)}) %all-to-all-start.2) | async-done | bytes 1048608 | tf_op jit(solution)/shard_map/all_to_all | solution.py:159
  64.4 34.8 %psum.7 = f32[2,256]{1,0:T(2,128)S(1)} all-reduce(f32[2,256]{1,0:T(2,128)S(1)} %add.148), channel_id=1, replica_groups=mesh['sites'=2,'blk'=16] {'blk'}, use_global_device_ids=true, to_apply=%region_14.15 | all-reduce | flops 512 | bytes 4096 | tf_op jit(solution)/shard_map/psum | solution.py:176
  100.3 0.8 convolution_bitcast_fusion.1
  101.0 0.8 convolution_bitcast_fusion
  101.8 0.9 copy.46
  (57 shorter events, 8.0 us)
Async XLA Ops:
  4.4 14.0 %all-to-all-start = ((s32[16,4,128]{2,1,0:T(4,128)}), s32[16,4,128]{2,1,0:T(4,128)S(1)}, u32[]{:S(2)}, u32[]{:S(2)}) async-start(s32[16,4,128]{2,1,0:T(4,128)} %bitcast.15), calls=%async_computation | async-start | bytes 65536 | tf_op jit(solution)/shard_map/all_to_all | solution.py:156
  18.4 11.4 %all-to-all-start.1 = ((bf16[64,8,128]{2,1,0:T(8,128)(2,1)}), bf16[64,8,128]{2,1,0:T(8,128)(2,1)S(1)}, u32[]{:S(2)}, u32[]{:S(2)}) async-start(bf16[64,8,128]{2,1,0:T(8,128)(2,1)} %bitcast.21), calls=%async_computation.1 | async-start | bytes 262144 | tf_op jit(solution)/shard_map/all_to_all | solution.py:155
  34.8 3.8 %copy-start.1 = (s32[2,4,8]{2,1,0:T(4,128)S(1)}, s32[2,4,8]{2,1,0:T(4,128)}, u32[]{:S(2)}) copy-start(s32[2,4,8]{2,1,0:T(4,128)} %param.14) | copy-start | bytes 772
  34.8 4.0 %copy-start.2 = (s32[2,16]{1,0:T(2,128)S(1)}, s32[2,16]{1,0:T(2,128)}, u32[]{:S(2)}) copy-start(s32[2,16]{1,0:T(2,128)} %param.13) | copy-start | bytes 388
  34.8 4.0 %copy-start.3 = (f32[2,4]{1,0:T(2,128)S(1)}, f32[2,4]{1,0:T(2,128)}, u32[]{:S(2)}) copy-start(f32[2,4]{1,0:T(2,128)} %param.15) | copy-start | bytes 100
  34.8 4.0 %copy-start = (s32[2,16,1]{1,2,0:T(1,128)S(1)}, s32[2,16,1]{1,2,0:T(1,128)}, u32[]{:S(2)}) copy-start(s32[2,16,1]{1,2,0:T(1,128)} %param.12) | copy-start | bytes 388
  34.8 26.7 %all-to-all-start.2 = ((bf16[64,8,1024]{2,1,0:T(8,128)(2,1)}), bf16[64,8,1024]{2,1,0:T(8,128)(2,1)S(1)}, u32[]{:S(2)}, u32[]{:S(2)}) async-start(bf16[64,8,1024]{2,1,0:T(8,128)(2,1)} %bitcast.24), calls=%async_computation.2 | async-start | bytes 2097152 | tf_op jit(solution)/shard_map/all_to_all | solution.py:159
where the time goes:
time: 103 us
  blocking collectives  34.8 us (34%)
  waiting for transfers between devices  29.7 us (29%)
  starting transfers between devices  14.7 us (14%)
  local copies, waits for them, and re-layouts  11.4 us (11%)
  other arithmetic  7.13 us (7%)
  matrix products  4.04 us (4%)
    psum x1, blocking collectives, local(): total_power = lax.psum(power_sum, 'blk')  34.8 us
    all_to_all x1, waiting for transfers between devices, local(): lax.all_to_all(partials, 'blk', split_axis=0, concat_axis=0, tiled=True)  19.8 us
    all_to_all x1, starting transfers between devices, local(): lax.all_to_all(onset_all, 'blk', split_axis=0, concat_axis=0, tiled=True)  7.39 us
    all_to_all x1, waiting for transfers between devices, local(): lax.all_to_all(slip_all, 'blk', split_axis=0, concat_axis=0, tiled=True)  6.72 us
    all_to_all x1, starting transfers between devices, local(): lax.all_to_all(partials, 'blk', split_axis=0, concat_axis=0, tiled=True)  3.8 us
    all_to_all x1, starting transfers between devices, local(): lax.all_to_all(slip_all, 'blk', split_axis=0, concat_axis=0, tiled=True)  3.51 us
    all_to_all x1, waiting for transfers between devices, local(): lax.all_to_all(onset_all, 'blk', split_axis=0, concat_axis=0, tiled=True)  3.1 us
    unnamed x12, local copies, waits for them, and re-layouts  2.67 us
  transfers between devices with their start and end apart: 3, of which 3 were waited for; matrix products, arithmetic and copies ran while one was open for 7% of the time, Pallas kernels for 0%

commit v1 on v0

v1 whole, which is shorter than its diff:
```python
import functools
import math

import jax
import jax.numpy as jnp
import numpy as np
from jax import lax
from jax.experimental import pallas as pl
from jax.experimental.pallas import tpu as pltpu
from jax.sharding import PartitionSpec as P

BIN_LAG = 9
ONSET_BINS = 4
CAPACITY = 2
SAMPLES = 512
F32 = jnp.float32
BF16 = jnp.bfloat16


def phase_table(freqs, rows):
    turns = np.arange(ONSET_BINS)[:, None] * BIN_LAG * np.arange(freqs)[None, :] % SAMPLES
    angles = 2.0 * math.pi / SAMPLES * turns
    both = np.stack([np.cos(angles), np.sin(angles)])
    return np.repeat(both.reshape(2 * ONSET_BINS, freqs), rows, axis=0).astype(np.float32)


def inverse_table(freqs):
    frequency = np.arange(freqs)
    angles = 2.0 * math.pi / SAMPLES * (frequency[:, None] * np.arange(SAMPLES)[None, :] % SAMPLES)
    weight = np.where(frequency == 0, 1.0 / SAMPLES, 2.0 / SAMPLES)[:, None]
    return np.concatenate([weight * np.cos(angles), -weight * np.sin(angles)]).astype(np.float32)


def column(row):
    n = row.shape[1]
    diag = lax.broadcasted_iota(jnp.int32, (n, n), 0) == lax.broadcasted_iota(jnp.int32, (n, n), 1)
    return jnp.sum(jnp.where(diag, jnp.broadcast_to(row, (n, n)), 0.0), axis=1, keepdims=True)


def kernel(
    dims,
    green_ref,
    slip_ref,
    onset_ref,
    helper_ref,
    rupture_ref,
    shift_ref,
    rate_ref,
    phase_ref,
    inverse_ref,
    out_ref,
    power_ref,
    gat,
    rows_ref,
    acc,
    cos_ref,
    sin_ref,
    inv,
    pw,
    local_sem,
    ring_s,
    ring_r,
    sib_s,
    sib_r,
    pw_s,
    pw_r,
):
    devices, batches, items, variations, rupts, comps, freqs = dims
    subs = green_ref.shape[0]
    half_rows = subs // 2
    chips = devices // 2
    me = lax.axis_index("blk")
    core = me % 2
    chip = me // 2
    folded = chips % 2 == 0

    def chip_at(pos):
        if not folded:
            return pos
        back = pos // (chips // 2)
        return (1 - back) * 2 * pos + back * (2 * (chips - 1 - pos) + 1)

    if folded:
        odd = chip % 2
        q = (1 - odd) * (chip // 2) + odd * (chips - 1 - chip // 2)
    else:
        q = chip
    right = chip_at((q + 1) % chips) * 2 + core
    left = chip_at((q + chips - 1) % chips) * 2 + core
    sibling = chip * 2 + (1 - core)

    def chunk(side, j, shift, which):
        step = j // 2 + shift
        pos = (q + chips - step) % chips if side == 0 else (q + step) % chips
        half = j % 2 if side == 0 else 1 - j % 2
        return gat.at[pos * 2 + which, pl.ds(pl.multiple_of(half * half_rows, half_rows), half_rows)]

    def ring(side, j, shift):
        piece = chunk(side, j, shift, core)
        return pltpu.make_async_remote_copy(
            src_ref=piece,
            dst_ref=piece,
            send_sem=ring_s.at[side, j],
            recv_sem=ring_r.at[side, j],
            device_id={"blk": right if side == 0 else left},
            device_id_type=pl.DeviceIdType.MESH,
        )

    def sib(side, j, which):
        piece = chunk(side, j, 1, which)
        return pltpu.make_async_remote_copy(
            src_ref=piece,
            dst_ref=piece,
            send_sem=sib_s.at[side, j],
            recv_sem=sib_r.at[side, j],
            device_id={"blk": sibling},
            device_id_type=pl.DeviceIdType.MESH,
        )

    def sib_own(half, which):
        piece = gat.at[q * 2 + which, pl.ds(half * half_rows, half_rows)]
        return pltpu.make_async_remote_copy(
            src_ref=piece,
            dst_ref=piece,
            send_sem=sib_s.at[half, chips - 1],
            recv_sem=sib_r.at[half, chips - 1],
            device_id={"blk": sibling},
            device_id_type=pl.DeviceIdType.MESH,
        )

    own = pltpu.make_async_copy(green_ref, gat.at[q * 2 + core], local_sem.at[0])
    own.start()
    table = pltpu.make_async_copy(inverse_ref, inv, local_sem.at[1])
    table.start()
    barrier = pltpu.get_barrier_semaphore()

    @pl.loop(1, devices)
    def _(o):
        pl.semaphore_signal(
            barrier, inc=1, device_id={"blk": (me + o) % devices}, device_id_type=pl.DeviceIdType.MESH
        )

    pl.semaphore_wait(barrier, devices - 1)
    own.wait()
    for j in range(min(2, chips - 1)):
        for side in range(2):
            ring(side, j, 0).start()
    for half in range(2):
        sib_own(half, core).start()

    total = batches * items
    lanes = total * variations
    slots = batches * CAPACITY
    group = ONSET_BINS * variations
    cols = subs
    helper_col = jnp.concatenate([column(helper_ref[b].astype(F32)) for b in range(batches)], axis=0)
    rupture_col = jnp.concatenate(
        [column(rupture_ref[b : b + 1, :].astype(F32)) for b in range(batches)], axis=0
    )
    lane = lax.broadcasted_iota(jnp.int32, (total, lanes), 1)
    lane_item = lane // variations
    item = lax.broadcasted_iota(jnp.int32, (total, lanes), 0)
    helper_lane = jnp.sum(jnp.where(lane_item == item, helper_col, 0.0), axis=0, keepdims=True)
    earlier = jnp.logical_and(item < lane_item, item // items == lane_item // items)
    same = jnp.logical_and(helper_col == helper_lane, earlier)
    rank = jnp.sum(jnp.where(same, 1.0, 0.0), axis=0, keepdims=True)
    lane1 = lax.broadcasted_iota(jnp.int32, (1, lanes), 1)
    batch1 = lane1 // (variations * items)
    key = (helper_lane.astype(jnp.int32) * slots + batch1 * CAPACITY + rank.astype(jnp.int32)) * variations
    key = key + lane1 % variations
    target = lax.broadcasted_iota(jnp.int32, (slots * group, lanes), 0)
    target = target // group * variations + target % variations
    slip_rows = slip_ref[...].astype(F32).reshape(lanes, subs)
    rows_ref[:, :cols] = slip_rows.astype(BF16)
    onset_rows = onset_ref[...].astype(F32).reshape(total, 1, subs)
    onset_rows = jnp.broadcast_to(onset_rows, (total, variations, subs)).reshape(lanes, subs)
    rows_ref[:, cols : 2 * cols] = onset_rows.astype(BF16)
    rupture_rows = jnp.broadcast_to(rupture_col, (total, 128)).reshape(total, 1, 128)
    rupture_rows = jnp.broadcast_to(rupture_rows, (total, variations, 128)).reshape(lanes, 128)
    rows_ref[:, 2 * cols :] = rupture_rows.astype(BF16)
    row_bin = lax.broadcasted_iota(jnp.int32, (slots * group, subs), 0) % group // variations
    row_bin = row_bin.astype(F32)
    acc[...] = jnp.zeros_like(acc)

    def compute(pos, which):
        h = chip_at(pos) * 2 + which
        pick = jnp.where(key - h * (slots * variations) == target, 1.0, 0.0).astype(BF16)
        picked = jnp.dot(pick, rows_ref[...], preferred_element_type=F32)
        masked = jnp.where(picked[:, cols : 2 * cols] == row_bin, picked[:, :cols], 0.0).astype(BF16)
        rupture = picked[:, 2 * cols :]
        for c in range(comps):
            lo = c * 2 * freqs
            summed = jnp.dot(
                masked, gat[pos * 2 + which, :, lo : lo + 2 * freqs], preferred_element_type=F32
            )
            for slot in range(slots):
                real_part = summed[slot * group : slot * group + variations, :freqs]
                imag_part = summed[slot * group : slot * group + variations, freqs:]
                real_sum, imag_sum = real_part, imag_part
                for k in range(1, ONSET_BINS):
                    at = slot * group + k * variations
                    real_part = summed[at : at + variations, :freqs]
                    imag_part = summed[at : at + variations, freqs:]
                    cos_k = phase_ref[k * variations : (k + 1) * variations, :]
                    s = (ONSET_BINS + k) * variations
                    sin_k = phase_ref[s : s + variations, :]
                    real_sum = real_sum + (cos_k * real_part + sin_k * imag_part)
                    imag_sum = imag_sum + (cos_k * imag_part - sin_k * real_part)
                both = jnp.concatenate([real_sum, imag_sum], axis=1).astype(BF16).astype(F32)
                named = rupture[slot * group : slot * group + variations, :]
                named = jnp.concatenate([named] * (2 * freqs // 128), axis=1)
                b = slot // CAPACITY
                for r in range(rupts):
                    base = (b * rupts + r) * variations
                    acc[base : base + variations, lo : lo + 2 * freqs] += jnp.where(
                        named == float(r), both, 0.0
                    )

    def arrive(j):
        for side in range(2):
            ring(side, j, 1).wait_recv()

            @pl.when(j + 2 <= chips - 2)
            def _():
                ring(side, j + 2, 0).start()

            sib(side, j, core).start()

    def sib_wait(j):
        for side in range(2):
            sib(side, j, 1 - core).wait_recv()

    def several(d, count):
        @pl.loop(0, count)
        def _(t):
            step = d - t // 2
            other = t // 2
            pos = (q + chips + (2 * (t % 2) - 1) * step) % chips
            compute(pos, core + other - 2 * core * other)

    frequency = lax.broadcasted_iota(jnp.int32, (variations, freqs), 1)
    for b in range(batches):
        for r in range(rupts):
            shift = column(shift_ref[b, r : r + 1, :].astype(F32)).astype(jnp.int32)
            turns = shift * frequency % SAMPLES
            angles = 2.0 * math.pi / SAMPLES * turns.astype(F32)
            base = (b * rupts + r) * variations
            cos_ref[base : base + variations, :] = jnp.cos(angles)
            sin_ref[base : base + variations, :] = jnp.sin(angles)

    compute(q, core)
    most = (chips - 1) // 2
    arrive(0)
    arrive(1)
    for half in range(2):
        sib_own(half, 1 - core).wait_recv()
    several(1, 3)

    @pl.loop(2, most + 1)
    def _(d):
        arrive(2 * d - 2)
        arrive(2 * d - 1)
        sib_wait(2 * d - 4)
        sib_wait(2 * d - 3)
        several(d, 4)

    if folded:
        arrive(chips - 2)
    sib_wait(2 * most - 2)
    sib_wait(2 * most - 1)
    if folded:
        compute((q + chips // 2) % chips, core)
    compute((q + chips - most) % chips, 1 - core)
    compute((q + most) % chips, 1 - core)
    if folded:
        sib_wait(chips - 2)
        compute((q + chips // 2) % chips, 1 - core)

    for c in range(comps):
        lo = c * 2 * freqs
        energy = jnp.zeros((variations, freqs), F32)
        for b in range(batches):
            for r in range(rupts):
                base = (b * rupts + r) * variations
                real_part = acc[base : base + variations, lo : lo + freqs]
                imag_part = acc[base : base + variations, lo + freqs : lo + 2 * freqs]
                square = real_part * real_part + imag_part * imag_part
                energy = energy + rate_ref[b : b + 1, r : r + 1] * square
        pw[me, c : c + 1, :] = jnp.sum(energy, axis=0, keepdims=True) * (1.0 / variations)

    def power_copy(o):
        return pltpu.make_async_remote_copy(
            src_ref=pw.at[me],
            dst_ref=pw.at[me],
            send_sem=pw_s.at[o],
            recv_sem=pw_r.at[o],
            device_id={"blk": (me + o) % devices},
            device_id_type=pl.DeviceIdType.MESH,
        )

    def power_arrival(o):
        slot = pw.at[(me + devices - o) % devices]
        return pltpu.make_async_remote_copy(
            src_ref=slot,
            dst_ref=slot,
            send_sem=pw_s.at[o],
            recv_sem=pw_r.at[o],
            device_id={"blk": (me + o) % devices},
            device_id_type=pl.DeviceIdType.MESH,
        )

    @pl.loop(1, devices)
    def _(o):
        power_copy(o).start()

    table.wait()
    cos_shift = cos_ref[...]
    sin_shift = sin_ref[...]
    for c in range(comps):
        lo = c * 2 * freqs
        real_part = acc[:, lo : lo + freqs]
        imag_part = acc[:, lo + freqs : lo + 2 * freqs]
        shifted = jnp.concatenate(
            [
                real_part * cos_shift + imag_part * sin_shift,
                imag_part * cos_shift - real_part * sin_shift,
            ],
            axis=1,
        )
        out_ref[:, c * SAMPLES : (c + 1) * SAMPLES] = jnp.dot(
            shifted, inv[...], precision=lax.Precision.HIGHEST, preferred_element_type=F32
        )

    @pl.loop(1, devices)
    def _(o):
        power_arrival(o).wait_recv()

    power_ref[...] = jnp.log(jnp.sum(pw[...], axis=0))

    @pl.loop(1, devices)
    def _(o):
        power_copy(o).wait_send()

    @pl.loop(0, chips - 1)
    def _(j):
        for side in range(2):
            ring(side, j, 0).wait_send()
            sib(side, j, core).wait_send()

    for half in range(2):
        sib_own(half, core).wait_send()


def local(green, slip, onset_bin, item_helper, item_rupture, base_shift, rupture_rate):
    devices = lax.axis_size("blk")
    subs, comps, _, freqs = green.shape
    batches, items, variations, _ = slip.shape
    rupts = base_shift.shape[1]
    width = comps * 2 * freqs
    rows = batches * rupts * variations
    chips = devices // 2
    dims = (devices, batches, items, variations, rupts, comps, freqs)
    gathered = devices * subs * width * 2
    vmem = pl.BlockSpec(memory_space=pltpu.VMEM)
    anywhere = pl.BlockSpec(memory_space=pl.ANY)
    seismo, power = pl.pallas_call(
        functools.partial(kernel, dims),
        out_shape=(
            jax.ShapeDtypeStruct((rows, comps * SAMPLES), F32),
            jax.ShapeDtypeStruct((comps, freqs), F32),
        ),
        in_specs=[anywhere, vmem, vmem, vmem, vmem, vmem, vmem, vmem, anywhere],
        out_specs=(vmem, vmem),
        scratch_shapes=[
            pltpu.VMEM((devices, subs, width), BF16),
            pltpu.VMEM((batches * items * variations, 2 * subs + 128), BF16),
            pltpu.VMEM((rows, width), F32),
            pltpu.VMEM((rows, freqs), F32),
            pltpu.VMEM((rows, freqs), F32),
            pltpu.VMEM((2 * freqs, SAMPLES), F32),
            pltpu.VMEM((devices, comps, freqs), F32),
            pltpu.SemaphoreType.DMA((2,)),
            pltpu.SemaphoreType.DMA((2, chips)),
            pltpu.SemaphoreType.DMA((2, chips)),
            pltpu.SemaphoreType.DMA((2, chips)),
            pltpu.SemaphoreType.DMA((2, chips)),
            pltpu.SemaphoreType.DMA((devices,)),
            pltpu.SemaphoreType.DMA((devices,)),
        ],
        compiler_params=pltpu.CompilerParams(
            collective_id=0, has_side_effects=True, vmem_limit_bytes=min(60, 20 + (gathered >> 20)) << 20
        ),
    )(
        green.reshape(subs, width),
        slip,
        onset_bin,
        item_helper.reshape(batches, 1, items),
        item_rupture,
        base_shift,
        rupture_rate,
        jnp.asarray(phase_table(freqs, variations)),
        jnp.asarray(inverse_table(freqs)),
    )
    return seismo.reshape(batches, rupts, variations, comps, SAMPLES), power


def solution(mesh):
    placed = (
        P(("sites", "blk"), None, None, None),
        P(None, "blk", None, None),
        P(None, "blk", None),
        P(None, "blk", None),
        P(None, "blk"),
        P(None, "blk", None),
        P(None, "blk"),
    )
    return jax.shard_map(
        local,
        mesh=mesh,
        in_specs=placed,
        out_specs=(P(None, ("sites", "blk"), None, None, None), P("sites", None)),
        check_vma=False,
    )
```

time: 103 us -> 38.1 us (0.37)
  blocking collectives: 34.8 us -> 0 us
  Pallas kernels: 0 us -> 33.2 us
  waiting for transfers between devices: 29.7 us -> 0 us
  starting transfers between devices: 14.7 us -> 0 us
  local copies, waits for them, and re-layouts: 11.4 us -> 3.92 us
  other arithmetic: 7.13 us -> 0 us
  matrix products: 4.04 us -> 0 us
    psum x1 -> x0, blocking collectives: 34.8 us -> none  [local(): total_power = lax.psum(power_sum, 'blk')]
    pallas_call x0 -> x1, Pallas kernels: none -> 33.2 us  [local(): pl.pallas_call(functools.partial(kernel, dims), out_shape=(jax.ShapeDtype...]
    all_to_all x3 -> x0, waiting for transfers between devices: 29.7 us -> none  [the longest x1 19.8 us: local(): lax.all_to_all(partials, 'blk', split_axis=0, concat_axis=0, tiled=True)]
    all_to_all x3 -> x0, starting transfers between devices: 14.7 us -> none  [the longest x1 7.39 us: local(): lax.all_to_all(onset_all, 'blk', split_axis=0, concat_axis=0, tiled=True)]
    dot_general x6 -> x0, matrix products: 4.04 us -> none  [the longest x2 1.51 us: finish_batch(): jnp.dot(shifted.reshape(rupt_count * VARIATIONS * COMPS, 2 * FREQS), inve...]
    scatter x4 -> x0, local copies, waits for them, and re-layouts: 3.62 us -> none  [the longest x2 2.03 us: local(): jnp.zeros((stride,) + slip_tail, slip.dtype).at[slot_index]]
    mul x5 -> x0, other arithmetic: 2.39 us -> none  [the longest x1 2.12 us: inverse_table(): -weight * jnp.sin(angles)]
    reduce_sum x5 -> x0, other arithmetic: 1.73 us -> none  [the longest x2 1.38 us: one_group(): jnp.sum(cos_rows * summed[:, :, :, :, 0] + sin_rows * summed[:, :, :, :,...]
  transfers between devices with their start and end apart: 3 -> 0, of which waited for: 3 -> 0; matrix products, arithmetic and copies ran while one was open for 7% -> 0% of each run, Pallas kernels for 0% -> 0%
where the time goes in v1:
time: 38.1 us; the launch traced here: 37.9 us
  Pallas kernels  33.2 us (87%)
  local copies, waits for them, and re-layouts  3.92 us (10%)
  between operations  0.76 us (2%)
    pallas_call x1, Pallas kernels, local(): pl.pallas_call(functools.partial(kernel, dims), out_shape=(jax.ShapeDtype...  33.2 us
    unnamed x18, local copies, waits for them, and re-layouts  2.74 us
    reshape x1, local copies, waits for them, and re-layouts, local(): green.reshape(subs, width)  1.19 us

profile of v1, /device:TPU:0, one launch (start us, length us, event | category | flops | bytes accessed | tf_op | source)
XLA Modules:
  0.0 37.9 jit_solution(11030749704867676810)
XLA Ops:
  0.6 0.0 copy-start.1
  0.6 0.0 copy-start.2
  0.7 0.0 copy-start.3
  0.7 0.0 copy-start.4
  0.7 0.0 copy-start.5
  0.7 0.0 copy-start.6
  0.7 0.0 copy-start.7
  0.7 1.2 %reshape.13.green_ref = bf16[128,1024]{1,0:T(8,128)(2,1)S(1)} reshape(bf16[128,2,2,256]{3,2,1,0:T(2,128)(2,1)} %param.9) | data formatting | bytes 524288 | tf_op jit(solution)/shard_map/reshape | solution.py:394
  1.9 0.0 copy-done.1
  1.9 0.0 copy-done.2
  1.9 0.0 copy-done.3
  1.9 0.0 copy-done.4
  1.9 0.0 copy-done.5
  1.9 0.0 copy-done.6
  2.0 0.0 copy-done.7
  2.0 0.0 copy-start
  2.0 1.2 %copy-done = f32[512,512]{1,0:T(8,128)S(1)} copy-done((f32[512,512]{1,0:T(8,128)S(1)}, f32[512,512]{1,0:T(8,128)}, u32[]{:S(2)}) %copy-start) | copy-done | bytes 1048600
  3.2 33.2 %shard_map.104 = (f32[64,1024]{1,0:T(8,128)S(1)}, f32[2,256]{1,0:T(2,128)S(1)}) custom-call(bf16[128,1024]{1,0:T(8,128)(2,1)S(1)} %reshape.13.green_ref, bf16[2,16,8,128]{3,2,1,0:T(8,128)(2,1)S(1)} %copy-done.1, s32[2,16,128]{2,1,0:T(8,128)S(1)} %copy-done.3, s32[2,1,16]{2,1,0:T(1,128)S(1)} %bitcast.5, s32[2,16]{1,0:T(2,128)S(1)} %copy-done.6, ...), custom_call_target="tpu_custom_call" | custom-call | tf_op jit(solution)/shard_map/pallas_call | solution.py:366
  36.4 0.9 %copy.12 = f32[2,4,8,2,512]{4,3,2,1,0:T(2,128)} copy(f32[2,4,8,2,512]{4,2,3,1,0:T(8,128)S(1)} %bitcast.4) | data formatting | bytes 524288
  37.3 0.6 %copy.14 = f32[2,256]{1,0:T(2,128)} copy(f32[2,256]{1,0:T(2,128)S(1)} %get-tuple-element.11) | data formatting | bytes 4096
Async XLA Ops:
  0.6 1.3 %copy-start.1 = (bf16[2,16,8,128]{3,2,1,0:T(8,128)(2,1)S(1)}, bf16[2,16,8,128]{3,2,1,0:T(8,128)(2,1)}, u32[]{:S(2)}) copy-start(bf16[2,16,8,128]{3,2,1,0:T(8,128)(2,1)} %slip_ref.1) | copy-start | bytes 196612
  0.6 1.3 %copy-start.2 = (f32[64,256]{1,0:T(8,128)S(1)}, f32[64,256]{1,0:T(8,128)}, u32[]{:S(2)}) copy-start(f32[64,256]{1,0:T(8,128)} %constant.4.clone.phase_ref) | copy-start | bytes 196612
  0.7 1.3 %copy-start.3 = (s32[2,16,128]{2,1,0:T(8,128)S(1)}, s32[2,16,128]{2,1,0:T(8,128)}, u32[]{:S(2)}) copy-start(s32[2,16,128]{2,1,0:T(8,128)} %onset_ref.1) | copy-start | bytes 49156
  0.7 1.3 %copy-start.4 = (s32[2,4,8]{2,1,0:T(4,128)S(1)}, s32[2,4,8]{2,1,0:T(4,128)}, u32[]{:S(2)}) copy-start(s32[2,4,8]{2,1,0:T(4,128)} %shift_ref.1) | copy-start | bytes 772
  0.7 1.3 %copy-start.5 = (s32[2,16,1]{1,2,0:T(1,128)S(1)}, s32[2,16,1]{1,2,0:T(1,128)}, u32[]{:S(2)}) copy-start(s32[2,16,1]{1,2,0:T(1,128)} %param.12) | copy-start | bytes 388
  0.7 1.3 %copy-start.6 = (s32[2,16]{1,0:T(2,128)S(1)}, s32[2,16]{1,0:T(2,128)}, u32[]{:S(2)}) copy-start(s32[2,16]{1,0:T(2,128)} %rupture_ref.1) | copy-start | bytes 388
  0.7 1.3 %copy-start.7 = (f32[2,4]{1,0:T(2,128)S(1)}, f32[2,4]{1,0:T(2,128)}, u32[]{:S(2)}) copy-start(f32[2,4]{1,0:T(2,128)} %rate_ref.1) | copy-start | bytes 100
  2.0 1.2 %copy-start = (f32[512,512]{1,0:T(8,128)S(1)}, f32[512,512]{1,0:T(8,128)}, u32[]{:S(2)}) copy-start(f32[512,512]{1,0:T(8,128)} %constant.5.clone.inverse_ref) | copy-start | bytes 3145732

commit v2 on v1

--- a/solution.py
+++ b/solution.py
@@ -22,13 +22,6 @@
     angles = 2.0 * math.pi / SAMPLES * turns
     both = np.stack([np.cos(angles), np.sin(angles)])
     return np.repeat(both.reshape(2 * ONSET_BINS, freqs), rows, axis=0).astype(np.float32)
-
-
-def inverse_table(freqs):
-    frequency = np.arange(freqs)
-    angles = 2.0 * math.pi / SAMPLES * (frequency[:, None] * np.arange(SAMPLES)[None, :] % SAMPLES)
-    weight = np.where(frequency == 0, 1.0 / SAMPLES, 2.0 / SAMPLES)[:, None]
-    return np.concatenate([weight * np.cos(angles), -weight * np.sin(angles)]).astype(np.float32)
 
 
 def column(row):
@@ -47,7 +40,6 @@
     shift_ref,
     rate_ref,
     phase_ref,
-    inverse_ref,
     out_ref,
     power_ref,
     gat,
@@ -55,7 +47,8 @@
     acc,
     cos_ref,
     sin_ref,
-    inv,
+    high,
+    low,
     pw,
     local_sem,
     ring_s,
@@ -130,17 +123,12 @@
 
     own = pltpu.make_async_copy(green_ref, gat.at[q * 2 + core], local_sem.at[0])
     own.start()
-    table = pltpu.make_async_copy(inverse_ref, inv, local_sem.at[1])
-    table.start()
     barrier = pltpu.get_barrier_semaphore()
 
-    @pl.loop(1, devices)
-    def _(o):
-        pl.semaphore_signal(
-            barrier, inc=1, device_id={"blk": (me + o) % devices}, device_id_type=pl.DeviceIdType.MESH
-        )
-
-    pl.semaphore_wait(barrier, devices - 1)
+    for peer in (right, left, sibling):
+        pl.semaphore_signal(barrier, inc=1, device_id={"blk": peer}, device_id_type=pl.DeviceIdType.MESH)
+
+    pl.semaphore_wait(barrier, 3)
     own.wait()
     for j in range(min(2, chips - 1)):
         for side in range(2):
@@ -256,6 +244,21 @@
         sib_own(half, 1 - core).wait_recv()
     several(1, 3)
 
+    strip = math.gcd(freqs, 32)
+
+    @pl.loop(0, freqs // strip)
+    def _(i):
+        first = pl.multiple_of(i * strip, strip)
+        f = lax.broadcasted_iota(jnp.int32, (strip, SAMPLES), 0) + first
+        turns = f * lax.broadcasted_iota(jnp.int32, (strip, SAMPLES), 1) % SAMPLES
+        angles = 2.0 * math.pi / SAMPLES * turns.astype(F32)
+        weight = jnp.where(f == 0, 1.0 / SAMPLES, 2.0 / SAMPLES)
+        for values, base in ((weight * jnp.cos(angles), 0), (-weight * jnp.sin(angles), freqs)):
+            rounded = values.astype(BF16)
+            at = pl.ds(pl.multiple_of(base + first, strip), strip)
+            high[at, :] = rounded
+            low[at, :] = (values - rounded.astype(F32)).astype(BF16)
+
     @pl.loop(2, most + 1)
     def _(d):
         arrive(2 * d - 2)
@@ -264,15 +267,13 @@
         sib_wait(2 * d - 3)
         several(d, 4)
 
-    if folded:
-        arrive(chips - 2)
     sib_wait(2 * most - 2)
     sib_wait(2 * most - 1)
-    if folded:
-        compute((q + chips // 2) % chips, core)
     compute((q + chips - most) % chips, 1 - core)
     compute((q + most) % chips, 1 - core)
     if folded:
+        arrive(chips - 2)
+        compute((q + chips // 2) % chips, core)
         sib_wait(chips - 2)
         compute((q + chips // 2) % chips, 1 - core)
 
@@ -313,23 +314,31 @@
     def _(o):
         power_copy(o).start()
 
-    table.wait()
     cos_shift = cos_ref[...]
     sin_shift = sin_ref[...]
+    shifted = []
     for c in range(comps):
         lo = c * 2 * freqs
         real_part = acc[:, lo : lo + freqs]
         imag_part = acc[:, lo + freqs : lo + 2 * freqs]
-        shifted = jnp.concatenate(
-            [
-                real_part * cos_shift + imag_part * sin_shift,
-                imag_part * cos_shift - real_part * sin_shift,
-            ],
-            axis=1,
-        )
-        out_ref[:, c * SAMPLES : (c + 1) * SAMPLES] = jnp.dot(
-            shifted, inv[...], precision=lax.Precision.HIGHEST, preferred_element_type=F32
-        )
+        shifted.append(
+            jnp.concatenate(
+                [
+                    real_part * cos_shift + imag_part * sin_shift,
+                    imag_part * cos_shift - real_part * sin_shift,
+                ],
+                axis=1,
+            )
+        )
+    shifted = jnp.concatenate(shifted, axis=0)
+    shifted_high = shifted.astype(BF16)
+    shifted_low = (shifted - shifted_high.astype(F32)).astype(BF16)
+    seismo = jnp.dot(shifted_high, high[...], preferred_element_type=F32)
+    seismo = seismo + jnp.dot(shifted_low, high[...], preferred_element_type=F32)
+    seismo = seismo + jnp.dot(shifted_high, low[...], preferred_element_type=F32)
+    count = acc.shape[0]
+    for c in range(comps):
+        out_ref[:, c * SAMPLES : (c + 1) * SAMPLES] = seismo[c * count : (c + 1) * count, :]
 
     @pl.loop(1, devices)
     def _(o):
@@ -369,7 +378,7 @@
             jax.ShapeDtypeStruct((rows, comps * SAMPLES), F32),
             jax.ShapeDtypeStruct((comps, freqs), F32),
         ),
-        in_specs=[anywhere, vmem, vmem, vmem, vmem, vmem, vmem, vmem, anywhere],
+        in_specs=[anywhere, vmem, vmem, vmem, vmem, vmem, vmem, vmem],
         out_specs=(vmem, vmem),
         scratch_shapes=[
             pltpu.VMEM((devices, subs, width), BF16),
@@ -377,9 +386,10 @@
             pltpu.VMEM((rows, width), F32),
             pltpu.VMEM((rows, freqs), F32),
             pltpu.VMEM((rows, freqs), F32),
-            pltpu.VMEM((2 * freqs, SAMPLES), F32),
+            pltpu.VMEM((2 * freqs, SAMPLES), BF16),
+            pltpu.VMEM((2 * freqs, SAMPLES), BF16),
             pltpu.VMEM((devices, comps, freqs), F32),
-            pltpu.SemaphoreType.DMA((2,)),
+            pltpu.SemaphoreType.DMA((1,)),
             pltpu.SemaphoreType.DMA((2, chips)),
             pltpu.SemaphoreType.DMA((2, chips)),
             pltpu.SemaphoreType.DMA((2, chips)),
@@ -399,7 +409,6 @@
         base_shift,
         rupture_rate,
         jnp.asarray(phase_table(freqs, variations)),
-        jnp.asarray(inverse_table(freqs)),
     )
     return seismo.reshape(batches, rupts, variations, comps, SAMPLES), power
 

time: 38.1 us -> 36.7 us (0.963)
  local copies, waits for them, and re-layouts: 3.92 us -> 2.7 us
    unnamed x18 -> x16, local copies, waits for them, and re-layouts: 2.74 us -> 1.52 us
where the time goes in v2:
time: 36.7 us; the launch traced here: 36.5 us
  Pallas kernels  33.1 us (90%)
  local copies, waits for them, and re-layouts  2.7 us (7%)
  between operations  0.75 us (2%)
    pallas_call x1, Pallas kernels, local(): pl.pallas_call(functools.partial(kernel, dims), out_shape=(jax.ShapeDtype...  33.1 us
    unnamed x16, local copies, waits for them, and re-layouts  1.52 us
    reshape x1, local copies, waits for them, and re-layouts, local(): green.reshape(subs, width)  1.19 us

profile of v2, /device:TPU:0, one launch (start us, length us, event | category | flops | bytes accessed | tf_op | source)
XLA Modules:
  0.0 36.5 jit_solution(14599839978833843419)
XLA Ops:
  0.6 0.0 copy-start
  0.6 0.0 copy-start.1
  0.7 0.0 copy-start.2
  0.7 0.0 copy-start.3
  0.7 0.0 copy-start.4
  0.7 0.0 copy-start.5
  0.7 0.0 copy-start.6
  0.7 1.2 %reshape.13.green_ref = bf16[128,1024]{1,0:T(8,128)(2,1)S(1)} reshape(bf16[128,2,2,256]{3,2,1,0:T(2,128)(2,1)} %param.8) | data formatting | bytes 524288 | tf_op jit(solution)/shard_map/reshape | solution.py:404
  1.9 0.0 copy-done
  1.9 0.0 copy-done.1
  1.9 0.0 copy-done.2
  1.9 0.0 copy-done.3
  1.9 0.0 copy-done.4
  1.9 0.0 copy-done.5
  2.0 0.0 copy-done.6
  2.0 33.1 %shard_map.95 = (f32[64,1024]{1,0:T(8,128)S(1)}, f32[2,256]{1,0:T(2,128)S(1)}) custom-call(bf16[128,1024]{1,0:T(8,128)(2,1)S(1)} %reshape.13.green_ref, bf16[2,16,8,128]{3,2,1,0:T(8,128)(2,1)S(1)} %copy-done, s32[2,16,128]{2,1,0:T(8,128)S(1)} %copy-done.2, s32[2,1,16]{2,1,0:T(1,128)S(1)} %bitcast.5, s32[2,16]{1,0:T(2,128)S(1)} %copy-done.5, ...), custom_call_target="tpu_custom_call" | custom-call | tf_op jit(solution)/shard_map/pallas_call | solution.py:375
  35.0 0.9 %copy.11 = f32[2,4,8,2,512]{4,3,2,1,0:T(2,128)} copy(f32[2,4,8,2,512]{4,2,3,1,0:T(8,128)S(1)} %bitcast.4) | data formatting | bytes 524288
  35.9 0.6 %copy.13 = f32[2,256]{1,0:T(2,128)} copy(f32[2,256]{1,0:T(2,128)S(1)} %get-tuple-element.11) | data formatting | bytes 4096
Async XLA Ops:
  0.6 1.3 %copy-start = (bf16[2,16,8,128]{3,2,1,0:T(8,128)(2,1)S(1)}, bf16[2,16,8,128]{3,2,1,0:T(8,128)(2,1)}, u32[]{:S(2)}) copy-start(bf16[2,16,8,128]{3,2,1,0:T(8,128)(2,1)} %slip_ref.1) | copy-start | bytes 196612
  0.6 1.3 %copy-start.1 = (f32[64,256]{1,0:T(8,128)S(1)}, f32[64,256]{1,0:T(8,128)}, u32[]{:S(2)}) copy-start(f32[64,256]{1,0:T(8,128)} %constant.2.clone.phase_ref) | copy-start | bytes 196612
  0.7 1.3 %copy-start.2 = (s32[2,16,128]{2,1,0:T(8,128)S(1)}, s32[2,16,128]{2,1,0:T(8,128)}, u32[]{:S(2)}) copy-start(s32[2,16,128]{2,1,0:T(8,128)} %onset_ref.1) | copy-start | bytes 49156
  0.7 1.3 %copy-start.3 = (s32[2,4,8]{2,1,0:T(4,128)S(1)}, s32[2,4,8]{2,1,0:T(4,128)}, u32[]{:S(2)}) copy-start(s32[2,4,8]{2,1,0:T(4,128)} %shift_ref.1) | copy-start | bytes 772
  0.7 1.3 %copy-start.4 = (s32[2,16,1]{1,2,0:T(1,128)S(1)}, s32[2,16,1]{1,2,0:T(1,128)}, u32[]{:S(2)}) copy-start(s32[2,16,1]{1,2,0:T(1,128)} %param.11) | copy-start | bytes 388
  0.7 1.3 %copy-start.5 = (s32[2,16]{1,0:T(2,128)S(1)}, s32[2,16]{1,0:T(2,128)}, u32[]{:S(2)}) copy-start(s32[2,16]{1,0:T(2,128)} %rupture_ref.1) | copy-start | bytes 388
  0.7 1.3 %copy-start.6 = (f32[2,4]{1,0:T(2,128)S(1)}, f32[2,4]{1,0:T(2,128)}, u32[]{:S(2)}) copy-start(f32[2,4]{1,0:T(2,128)} %rate_ref.1) | copy-start | bytes 100

commit v3 on v2

--- a/solution.py
+++ b/solution.py
@@ -170,12 +170,15 @@
     row_bin = row_bin.astype(F32)
     acc[...] = jnp.zeros_like(acc)
 
-    def compute(pos, which):
+    def prepare(pos, which):
         h = chip_at(pos) * 2 + which
         pick = jnp.where(key - h * (slots * variations) == target, 1.0, 0.0).astype(BF16)
         picked = jnp.dot(pick, rows_ref[...], preferred_element_type=F32)
         masked = jnp.where(picked[:, cols : 2 * cols] == row_bin, picked[:, :cols], 0.0).astype(BF16)
-        rupture = picked[:, 2 * cols :]
+        return masked, picked[:, 2 * cols :]
+
+    def finish(pos, which, prepared):
+        masked, rupture = prepared
         for c in range(comps):
             lo = c * 2 * freqs
             summed = jnp.dot(
@@ -204,6 +207,9 @@
                         named == float(r), both, 0.0
                     )
 
+    def compute(pos, which):
+        finish(pos, which, prepare(pos, which))
+
     def arrive(j):
         for side in range(2):
             ring(side, j, 1).wait_recv()
@@ -272,10 +278,12 @@
     compute((q + chips - most) % chips, 1 - core)
     compute((q + most) % chips, 1 - core)
     if folded:
+        across = (q + chips // 2) % chips
+        first, second = prepare(across, core), prepare(across, 1 - core)
         arrive(chips - 2)
-        compute((q + chips // 2) % chips, core)
+        finish(across, core, first)
         sib_wait(chips - 2)
-        compute((q + chips // 2) % chips, 1 - core)
+        finish(across, 1 - core, second)
 
     for c in range(comps):
         lo = c * 2 * freqs
@@ -295,22 +303,22 @@
             dst_ref=pw.at[me],
             send_sem=pw_s.at[o],
             recv_sem=pw_r.at[o],
-            device_id={"blk": (me + o) % devices},
+            device_id={"blk": lax.rem(me + o, devices)},
             device_id_type=pl.DeviceIdType.MESH,
         )
 
     def power_arrival(o):
-        slot = pw.at[(me + devices - o) % devices]
+        slot = pw.at[lax.rem(me + devices - o, devices)]
         return pltpu.make_async_remote_copy(
             src_ref=slot,
             dst_ref=slot,
             send_sem=pw_s.at[o],
             recv_sem=pw_r.at[o],
-            device_id={"blk": (me + o) % devices},
+            device_id={"blk": lax.rem(me + o, devices)},
             device_id_type=pl.DeviceIdType.MESH,
         )
 
-    @pl.loop(1, devices)
+    @pl.loop(1, devices, unroll=math.gcd(devices - 1, 5))
     def _(o):
         power_copy(o).start()
 
@@ -340,13 +348,13 @@
     for c in range(comps):
         out_ref[:, c * SAMPLES : (c + 1) * SAMPLES] = seismo[c * count : (c + 1) * count, :]
 
-    @pl.loop(1, devices)
+    @pl.loop(1, devices, unroll=math.gcd(devices - 1, 5))
     def _(o):
         power_arrival(o).wait_recv()
 
     power_ref[...] = jnp.log(jnp.sum(pw[...], axis=0))
 
-    @pl.loop(1, devices)
+    @pl.loop(1, devices, unroll=math.gcd(devices - 1, 5))
     def _(o):
         power_copy(o).wait_send()
 

time: 36.7 us -> 36.4 us (level)
  no operation moved by 1% of the time
where the time goes in v3:
time: 36.4 us; the launch traced here: 36.3 us
  Pallas kernels  32.8 us (90%)
  local copies, waits for them, and re-layouts  2.7 us (7%)
  between operations  0.75 us (2%)
    pallas_call x1, Pallas kernels, local(): pl.pallas_call(functools.partial(kernel, dims), out_shape=(jax.ShapeDtype...  32.8 us
    unnamed x16, local copies, waits for them, and re-layouts  1.52 us
    reshape x1, local copies, waits for them, and re-layouts, local(): green.reshape(subs, width)  1.19 us

profile of v3, /device:TPU:0, one launch (start us, length us, event | category | flops | bytes accessed | tf_op | source)
XLA Modules:
  0.0 36.3 jit_solution(5625853292041442622)
XLA Ops:
  0.6 0.0 copy-start
  0.6 0.0 copy-start.1
  0.7 0.0 copy-start.2
  0.7 0.0 copy-start.3
  0.7 0.0 copy-start.4
  0.7 0.0 copy-start.5
  0.7 0.0 copy-start.6
  0.7 1.2 %reshape.13.green_ref = bf16[128,1024]{1,0:T(8,128)(2,1)S(1)} reshape(bf16[128,2,2,256]{3,2,1,0:T(2,128)(2,1)} %param.8) | data formatting | bytes 524288 | tf_op jit(solution)/shard_map/reshape | solution.py:412
  1.9 0.0 copy-done
  1.9 0.0 copy-done.1
  1.9 0.0 copy-done.2
  1.9 0.0 copy-done.3
  1.9 0.0 copy-done.4
  1.9 0.0 copy-done.5
  2.0 0.0 copy-done.6
  2.0 32.8 %shard_map.95 = (f32[64,1024]{1,0:T(8,128)S(1)}, f32[2,256]{1,0:T(2,128)S(1)}) custom-call(bf16[128,1024]{1,0:T(8,128)(2,1)S(1)} %reshape.13.green_ref, bf16[2,16,8,128]{3,2,1,0:T(8,128)(2,1)S(1)} %copy-done, s32[2,16,128]{2,1,0:T(8,128)S(1)} %copy-done.2, s32[2,1,16]{2,1,0:T(1,128)S(1)} %bitcast.5, s32[2,16]{1,0:T(2,128)S(1)} %copy-done.5, ...), custom_call_target="tpu_custom_call" | custom-call | tf_op jit(solution)/shard_map/pallas_call | solution.py:383
  34.8 0.9 %copy.11 = f32[2,4,8,2,512]{4,3,2,1,0:T(2,128)} copy(f32[2,4,8,2,512]{4,2,3,1,0:T(8,128)S(1)} %bitcast.4) | data formatting | bytes 524288
  35.7 0.6 %copy.13 = f32[2,256]{1,0:T(2,128)} copy(f32[2,256]{1,0:T(2,128)S(1)} %get-tuple-element.11) | data formatting | bytes 4096
Async XLA Ops:
  0.6 1.3 %copy-start = (bf16[2,16,8,128]{3,2,1,0:T(8,128)(2,1)S(1)}, bf16[2,16,8,128]{3,2,1,0:T(8,128)(2,1)}, u32[]{:S(2)}) copy-start(bf16[2,16,8,128]{3,2,1,0:T(8,128)(2,1)} %slip_ref.1) | copy-start | bytes 196612
  0.6 1.3 %copy-start.1 = (f32[64,256]{1,0:T(8,128)S(1)}, f32[64,256]{1,0:T(8,128)}, u32[]{:S(2)}) copy-start(f32[64,256]{1,0:T(8,128)} %constant.2.clone.phase_ref) | copy-start | bytes 196612
  0.7 1.3 %copy-start.2 = (s32[2,16,128]{2,1,0:T(8,128)S(1)}, s32[2,16,128]{2,1,0:T(8,128)}, u32[]{:S(2)}) copy-start(s32[2,16,128]{2,1,0:T(8,128)} %onset_ref.1) | copy-start | bytes 49156
  0.7 1.3 %copy-start.3 = (s32[2,4,8]{2,1,0:T(4,128)S(1)}, s32[2,4,8]{2,1,0:T(4,128)}, u32[]{:S(2)}) copy-start(s32[2,4,8]{2,1,0:T(4,128)} %shift_ref.1) | copy-start | bytes 772
  0.7 1.3 %copy-start.4 = (s32[2,16,1]{1,2,0:T(1,128)S(1)}, s32[2,16,1]{1,2,0:T(1,128)}, u32[]{:S(2)}) copy-start(s32[2,16,1]{1,2,0:T(1,128)} %param.11) | copy-start | bytes 388
  0.7 1.3 %copy-start.5 = (s32[2,16]{1,0:T(2,128)S(1)}, s32[2,16]{1,0:T(2,128)}, u32[]{:S(2)}) copy-start(s32[2,16]{1,0:T(2,128)} %rupture_ref.1) | copy-start | bytes 388
  0.7 1.3 %copy-start.6 = (f32[2,4]{1,0:T(2,128)S(1)}, f32[2,4]{1,0:T(2,128)}, u32[]{:S(2)}) copy-start(f32[2,4]{1,0:T(2,128)} %rate_ref.1) | copy-start | bytes 100
